TPU v7x, 32 devices: a whole 2x2x4 slice. The times are simulated.
32 devices in a mesh: groups: 1, context: 8 (over y, x, core), span: 4 (over z).
Axes of the slice: x: 2, y: 2, z: 4, core: 2. Of those that a mesh axis runs over, the one named last changes fastest.
Arguments:
- raw_tokens: bfloat16 [1536, 2048], P(('groups', 'context'), 'span'), may hold values from -6 to 6
- keep: int32 [8, 32], P(('groups', 'context')), may hold values from -1 to 191, as said below
- attn_gain: float32 [2048], replicated, may hold values from 0.25 to 1.75
- query_weight: bfloat16 [2048, 4608], P(None, 'span'), may hold values from -5 to 5
- latent_weight: bfloat16 [2048, 576], P(None, 'span'), may hold values from -0.5 to 0.5
- kv_gain: float32 [512], replicated, may hold values from 0.25 to 1.75
- out_weight: bfloat16 [4096, 2048], P('span', 'context'), may hold values from -0.25 to 0.25
- moe_gain: float32 [2048], replicated, may hold values from 0.25 to 1.75
- expert_ids: int32 [256, 6], P(('groups', 'context', 'span')), may hold values from 0 to 15, all different within a row; in each aligned block of 8 rows (0 to 7, 8 to 15, ...) at most 6 rows name the same one
- gate_values: float32 [256, 6], P(('groups', 'context', 'span')), may hold values from 0.05 to 0.5
- expert_slot: int32 [16], replicated, may hold values from 0 to 15, each once
- expert_in: bfloat16 [32, 2, 2048, 704], P(('context', 'span')), may hold values from -0.125 to 0.125
- expert_out: bfloat16 [32, 704, 2048], P(('context', 'span')), may hold values from -0.15625 to 0.15625
Outputs:
- layer_out: bfloat16 [256, 2048], P(('groups', 'context', 'span'))
- latent_cache: bfloat16 [256, 576], P(('groups', 'context'))
Inputs may be any that keep to these rules, and one draw needn't show every extreme that they name: `keep`: row c lists the kept positions among the 192 raw tokens of span c in increasing order, then -1 in the empty entries; every span keeps 32 // 2 or more, and in every draw some span keeps 32. `expert_ids`: in each aligned block of 8 rows (the rows of one device) no expert is named more than 6 times, a bound that some block reaches. `expert_slot`: each stored slot holds exactly one routed expert.
All inputs are finite; a program needn't handle non-finite values.
Results may differ from a plain program's by a relative error of at most 0.013.
Values may be sent and summed in bfloat16 or wider, within the bound.
A program may use at most 64 MiB of HBM per device.

v0:
```python
import jax
import jax.numpy as jnp
from jax import lax
from jax.sharding import PartitionSpec as P

EPS = 1e-06
THETA = 50000.0
SCALE = 192.0 ** (-0.5)
NEGATIVE = -1e30


def rms_scale(values, gain):
    values = values.astype(jnp.float32)
    factor = lax.rsqrt(jnp.mean(values * values, axis=-1, keepdims=True) + EPS)
    return values * factor * gain


def rotary_tables(positions, rotary_width):
    half = rotary_width // 2
    freqs = THETA ** (-2.0 * jnp.arange(half, dtype=jnp.float32) / rotary_width)
    angles = positions.astype(jnp.float32)[:, None] * freqs[None, :]
    return (jnp.cos(angles), jnp.sin(angles))


def rotate(values, cosine, sine):
    half = values.shape[-1] // 2
    first = values[..., :half]
    second = values[..., half:]
    return jnp.concatenate(
        [first * cosine - second * sine, second * cosine + first * sine], axis=-1
    )


def piece_work(rows, expert_in, expert_out):
    shape = rows.shape
    flat = rows.reshape(-1, shape[-1])
    gate = jnp.dot(flat, expert_in[0, 0], preferred_element_type=jnp.float32)
    upper = jnp.dot(flat, expert_in[0, 1], preferred_element_type=jnp.float32)
    hidden = (jax.nn.silu(gate) * upper).astype(jnp.bfloat16)
    part = jnp.dot(hidden, expert_out[0], preferred_element_type=jnp.float32).astype(jnp.bfloat16)
    return part.reshape(shape)


def per_device(
    raw_tokens,
    keep,
    attn_gain,
    query_weight,
    latent_weight,
    kv_gain,
    out_weight,
    moe_gain,
    expert_ids,
    gate_values,
    expert_slot,
    expert_in,
    expert_out,
):
    kv_rank = kv_gain.shape[0]
    spans = lax.axis_size("span")
    latent_width = latent_weight.shape[1] * spans
    model_width = attn_gain.shape[0]
    keep_count = keep.shape[1]
    raw_rows = raw_tokens.shape[0]
    heads_here = query_weight.shape[1] // latent_width
    rows_dev = expert_ids.shape[0]
    choices_per_row = expert_ids.shape[1]
    experts = expert_slot.shape[0]
    capacity = max(2, min(rows_dev, (2 * rows_dev * choices_per_row + experts - 1) // experts))
    context_index = lax.axis_index("context")
    span_index = lax.axis_index("span")
    listing = keep[0]
    live = listing >= 0
    clamped = jnp.maximum(listing, 0)
    positions = context_index * raw_rows + clamped
    picked = jnp.take(raw_tokens, clamped, axis=0)
    picked = jnp.where(live[:, None], picked, jnp.zeros_like(picked))
    compact = lax.all_gather(picked, "span", axis=1, tiled=True)
    normed = rms_scale(compact, attn_gain).astype(jnp.bfloat16)
    cosine, sine = rotary_tables(positions, latent_width - kv_rank)
    query = jnp.dot(normed, query_weight, preferred_element_type=jnp.float32).reshape(
        keep_count, heads_here, latent_width
    )
    query = jnp.concatenate(
        [query[..., :kv_rank], rotate(query[..., kv_rank:], cosine[:, None, :], sine[:, None, :])],
        axis=-1,
    ).astype(jnp.bfloat16)
    latent_part = jnp.dot(normed, latent_weight, preferred_element_type=jnp.float32)
    latent = lax.all_gather(latent_part, "span", axis=1, tiled=True)
    cached = jnp.concatenate(
        [rms_scale(latent[:, :kv_rank], kv_gain), rotate(latent[:, kv_rank:], cosine, sine)],
        axis=-1,
    ).astype(jnp.bfloat16)
    live_flags = live.astype(jnp.bfloat16)
    query_ids = context_index * keep_count + jnp.arange(keep_count, dtype=jnp.int32)
    highest = jnp.full((heads_here, keep_count), NEGATIVE, jnp.float32)
    key_rows = lax.all_gather(cached, "context", axis=0, tiled=True)
    key_flags = lax.all_gather(live_flags, "context", axis=0, tiled=True)
    key_ids = jnp.arange(key_rows.shape[0], dtype=jnp.int32)
    allowed = (key_ids[None, :] <= query_ids[:, None]) & (key_flags[None, :] > 0)
    scores = jnp.einsum("qhd,kd->hqk", query, key_rows, preferred_element_type=jnp.float32) * SCALE
    scores = jnp.where(allowed[None], scores, NEGATIVE)
    raised = jnp.maximum(highest, jnp.max(scores, axis=-1))
    weights = jnp.where(allowed[None], jnp.exp(scores - raised[..., None]), 0.0)
    denominator = jnp.sum(weights, axis=-1)
    summed = jnp.einsum(
        "hqk,kd->hqd",
        weights.astype(jnp.bfloat16),
        key_rows[:, :kv_rank],
        preferred_element_type=jnp.float32,
    )
    highest, denominator, summed = (raised, denominator, summed)
    mixed = (summed / denominator[..., None]).astype(jnp.bfloat16)
    head_weights = lax.all_gather(out_weight, "context", axis=1, tiled=True).reshape(
        heads_here, kv_rank, model_width
    )
    attended = lax.psum_scatter(
        jnp.einsum("hqd,hdm->qm", mixed, head_weights, preferred_element_type=jnp.float32).astype(
            jnp.bfloat16
        ),
        "span",
        scatter_dimension=0,
        tiled=True,
    ).astype(jnp.float32)
    own_rows = lax.dynamic_slice_in_dim(compact, span_index * rows_dev, rows_dev, 0)
    resid = own_rows.astype(jnp.float32) + attended
    moe_in = rms_scale(resid, moe_gain).astype(jnp.bfloat16)
    expert_range = jnp.arange(experts, dtype=jnp.int32)
    chosen = expert_ids[:, :, None] == expert_range[None, None, :]
    slots = jnp.sum(jnp.where(chosen, expert_slot[None, None, :], 0), axis=-1).reshape(
        rows_dev * choices_per_row
    )
    member = (slots[:, None] == expert_range[None, :]).astype(jnp.int32)
    place = jnp.sum((jnp.cumsum(member, axis=0) - member) * member, axis=1)
    target = slots * capacity + place
    columns = jnp.arange(experts * capacity, dtype=jnp.int32)
    select = (
        (target[None, :] == columns[:, None])
        .astype(jnp.bfloat16)
        .reshape(experts * capacity, rows_dev, choices_per_row)
        .sum(axis=2)
    )
    outgoing = (
        jnp.dot(select, moe_in, preferred_element_type=jnp.float32)
        .astype(jnp.bfloat16)
        .reshape(experts, capacity, model_width)
    )
    copies = jnp.broadcast_to(outgoing[:, None], (experts, 2, capacity, model_width)).reshape(
        2 * experts, capacity, model_width
    )
    partial_rows = piece_work(
        lax.all_to_all(copies, ("context", "span"), split_axis=0, concat_axis=0, tiled=True),
        expert_in,
        expert_out,
    )
    gathered = lax.all_to_all(
        partial_rows, ("context", "span"), split_axis=0, concat_axis=0, tiled=True
    )
    returned = jnp.sum(
        gathered.reshape(experts, 2, capacity, model_width).astype(jnp.float32), axis=1
    )
    returned = returned.reshape(experts * capacity, model_width)
    hits = target.reshape(rows_dev, choices_per_row)[:, :, None] == columns[None, None, :]
    combine = jnp.sum(jnp.where(hits, gate_values[:, :, None], 0.0), axis=1)
    routed = jnp.dot(combine, returned, precision=lax.Precision.HIGHEST)
    row_live = lax.dynamic_slice_in_dim(live, span_index * rows_dev, rows_dev, 0)
    layer_out = jnp.where(row_live[:, None], resid + routed, 0.0).astype(jnp.bfloat16)
    return (layer_out, cached)


def solution(mesh):
    placed = (
        P(("groups", "context"), "span"),
        P(("groups", "context"), None),
        P(),
        P(None, "span"),
        P(None, "span"),
        P(),
        P("span", "context"),
        P(),
        P(("groups", "context", "span"), None),
        P(("groups", "context", "span"), None),
        P(),
        P(("context", "span"), None, None, None),
        P(("context", "span"), None, None),
    )
    return jax.shard_map(
        per_device,
        mesh=mesh,
        in_specs=placed,
        out_specs=(P(("groups", "context", "span"), None), P(("groups", "context"), None)),
        check_vma=False,
    )
```

profile of v0, /device:TPU:0, one launch (start us, length us, event | category | flops | bytes accessed | tf_op | source)
XLA Modules:
  0.0 183.7 jit_solution(15462238176401924297)
XLA Ops:
  7.2 0.0 copy-start
  7.2 0.0 copy-start.8
  7.2 0.0 all-gather.3.cloned.1.call-start
  7.3 0.7 all-gather.3.cloned.1.call-update
  8.0 0.0 reduce-scatter.2.cloned.1.call-start
  8.0 0.7 convert_bitcast_fusion
  8.8 1.6 gather_fusion
  10.4 0.7 broadcast_compare_fusion.1
  11.0 0.1 select_select_fusion
  11.1 15.1 %all_gather.15 = bf16[32,2048]{1,0:T(8,128)(2,1)S(1)} all-gather(bf16[32,512]{1,0:T(8,128)(2,1)S(1)} %select_select_fusion), channel_id=1, replica_groups=mesh['groups'=1,'context'=8,'span'=4] {'span'}, dimensions={1}, use_global_device_ids=true | all-gather | bytes 163840 | tf_op jit(solution)/shard_map/all_gather | solution.py:78
  26.2 0.1 fusion.32
  26.3 1.4 convolution_bitcast_fusion.1
  27.7 13.6 %all-gather = f32[4,144,32]{1,2,0:T(8,128)S(1)} all-gather(f32[1,144,32]{1,2,0:T(8,128)S(1)} %convolution_bitcast_fusion.1), channel_id=1, replica_groups=mesh['groups'=1,'context'=8,'span'=4] {'span'}, dimensions={0}, use_global_device_ids=true | all-gather | bytes 92160 | tf_op jit(solution)/shard_map/all_gather | solution.py:89
  41.4 0.1 copy.26
  41.5 0.1 reshape.238
  41.6 3.4 %fusion.43 = f32[32,1152]{1,0:T(8,128)S(1)} fusion(bf16[2048,1152]{1,0:T(8,128)(2,1)} %param.16, bf16[32,2048]{1,0:T(8,128)(2,1)S(1)} %all_gather.15, f32[2048]{0:T(1024)} %param.15, f32[32]{0:T(128)S(1)} %add_rsqrt_fusion.2), kind=kOutput, calls=%fused_computation.54 | convolution fusion | flops 151257088 | bytes 5005440 | tf_op jit(solution)/shard_map/dot_general | solution.py:81
  45.0 0.0 copy-start.3
  45.0 0.2 reshape.218
  45.2 0.6 copy.42
  45.9 0.1 copy.30
  46.0 0.0 copy-done.7
  46.0 0.2 select_reduce_fusion.2
  46.2 0.1 copy.31
  46.3 0.1 eq.58
  46.4 0.1 fusion.57
  46.5 0.1 reduce_window_sum.11
  46.5 0.2 select_reduce_fusion.1
  46.7 0.1 reduce_sum.91
  46.8 0.1 copy.32
  46.9 0.6 dynamic-slice.1
  48.2 0.2 dynamic-update-slice
  48.4 11.8 %all-reduce = bf16[256]{0:T(256)(128)(2,1)S(1)} all-reduce(bf16[256]{0:T(256)(128)(2,1)S(1)} %dynamic-update-slice), channel_id=1, replica_groups=mesh['groups'=1,'context'=8,'span'=4] {'context'}, use_global_device_ids=true, to_apply=%add | all-reduce | flops 256 | bytes 1024
  60.2 0.1 multiply_reduce_fusion.1
  60.4 0.1 multiply_cosine_fusion
  60.5 0.1 multiply_convert_fusion.1
  60.6 0.1 pad_maximum_fusion
  60.7 9.3 %all_gather.18 = bf16[256,576]{1,0:T(8,128)(2,1)S(1)} all-gather(bf16[32,576]{1,0:T(8,128)(2,1)S(1)} %pad_maximum_fusion), channel_id=1, replica_groups=mesh['groups'=1,'context'=8,'span'=4] {'context'}, dimensions={0}, use_global_device_ids=true | all-gather | bytes 331776 | tf_op jit(solution)/shard_map/all_gather | solution.py:97
  70.0 0.1 fusion.54
  70.1 0.1 fusion.68
  70.3 1.2 fusion.69
  71.4 0.2 fusion.41
  71.6 0.0 all-gather.3.cloned.1.call-done
  71.6 3.8 %fusion.11 = bf16[32,2048]{1,0:T(8,128)(2,1)} fusion(bf16[2,512,2048]{2,1,0:T(8,128)(2,1)} %bitcast.66, bf16[256,576]{1,0:T(8,128)(2,1)S(1)} %all_gather.18, f32[2,32]{1,0:T(2,128)S(1)} %fusion.41, f32[2,32,256]{2,1,0:T(8,128)S(1)} %get-tuple-element.19, f32[2,32]{1,0:T(2,128)S(1)} %broadcast_maximum_fusion, pred[32,256]{1,0:T(8,128)(4,1)S(1)} %fusion.54), kind=kOutput, calls=%fused_computation.12 | convolution fusion | flops 151175168 | bytes 4663296 | tf_op jit(solution)/shard_map/hqd,hdm->qm/dot_general | solution.py:118
  75.5 0.0 reduce-scatter.2.cloned.1.call-update
  75.5 0.1 fusion.60
  75.6 19.5 %reduce-scatter.2.cloned.1.call-done = bf16[8,2048]{1,0:T(8,128)(2,1)} async-done(((bf16[32,2048]{1,0:T(8,128)(2,1)}), bf16[8,2048]{1,0:T(8,128)(2,1)}) %reduce-scatter.2.cloned.1.call-update) | async-done | bytes 32784 | tf_op jit(solution)/shard_map/reduce_scatter | solution.py:117
  95.0 0.9 multiply_reduce_fusion
  95.9 1.8 convolution_convert_fusion
  97.8 1.1 broadcast_in_dim.125
  98.9 0.1 broadcast_in_dim.126
  99.0 27.8 %all_to_all.10 = bf16[32,6,2048]{2,1,0:T(8,128)(2,1)} all-to-all(bf16[32,6,2048]{2,1,0:T(8,128)(2,1)S(1)} %bitcast.67), channel_id=1, replica_groups=mesh['groups'=1,'context'=8,'span'=4] {'context','span'}, dimensions={0} | all-to-all | bytes 1572864 | tf_op jit(solution)/shard_map/all_to_all | solution.py:152
  126.8 2.2 %reshape.221 = bf16[192,2048]{1,0:T(8,128)(2,1)} reshape(bf16[32,6,2048]{2,1,0:T(8,128)(2,1)} %all_to_all.10) | data formatting | bytes 1572864 | tf_op jit(solution)/shard_map/reshape | solution.py:36
  129.0 3.9 %fusion.4 = f32[192,704]{1,0:T(8,128)} fusion(bf16[192,2048]{1,0:T(8,128)(2,1)} %reshape.221, bf16[1,2,2048,704]{2,3,1,0:T(8,128)(2,1)} %param.24), kind=kOutput, calls=%fused_computation.5 | convolution fusion | flops 553648128 | bytes 4210688 | tf_op jit(solution)/shard_map/dot_general | solution.py:37
  132.9 5.0 %fusion.8 = bf16[192,2048]{1,0:T(8,128)(2,1)} fusion(bf16[1,704,2048]{2,1,0:T(8,128)(2,1)S(1)} %copy-done, bf16[192,2048]{1,0:T(8,128)(2,1)} %reshape.221, bf16[1,2,2048,704]{2,3,1,0:T(8,128)(2,1)} %param.24, f32[192,704]{1,0:T(8,128)} %fusion.4), kind=kOutput, calls=%fused_computation.9 | convolution fusion | flops 1108500480 | bytes 7929856 | tf_op jit(solution)/shard_map/dot_general | solution.py:40
  137.9 2.2 %reshape.222 = bf16[32,6,2048]{2,1,0:T(8,128)(2,1)} reshape(bf16[192,2048]{1,0:T(8,128)(2,1)} %fusion.8) | data formatting | bytes 1572864 | tf_op jit(solution)/shard_map/reshape | solution.py:41
  140.2 4.6 %all-to-all-start.1 = ((bf16[32,6,2048]{2,1,0:T(8,128)(2,1)}), bf16[32,6,2048]{2,1,0:T(8,128)(2,1)}, u32[]{:S(2)}, u32[]{:S(2)}) async-start(bf16[32,6,2048]{2,1,0:T(8,128)(2,1)} %reshape.222), calls=%async_computation.2 | async-start | bytes 2097152 | tf_op jit(solution)/shard_map/all_to_all | solution.py:156
  144.8 0.0 copy-done.5
  144.8 0.1 copy.33
  144.9 0.1 dynamic-slice_bitcast_fusion
  144.9 0.1 select_reduce_fusion
  145.0 24.8 %all-to-all-done.1 = bf16[32,6,2048]{2,1,0:T(8,128)(2,1)} async-done(((bf16[32,6,2048]{2,1,0:T(8,128)(2,1)}), bf16[32,6,2048]{2,1,0:T(8,128)(2,1)}, u32[]{:S(2)}, u32[]{:S(2)}) %all-to-all-start.1) | async-done | bytes 786464 | tf_op jit(solution)/shard_map/all_to_all | solution.py:156
  169.8 2.6 %convert_reduce_fusion = f32[16,6,2048]{2,1,0:T(8,128)} fusion(bf16[32,6,2048]{2,1,0:T(8,128)(2,1)} %all-to-all-done.1), kind=kLoop, calls=%fused_computation.16 | loop fusion | flops 589824 | bytes 1572864 | tf_op jit(solution)/shard_map/reduce_sum | solution.py:159
  172.4 2.2 %reshape.223 = f32[96,2048]{1,0:T(8,128)} reshape(f32[16,6,2048]{2,1,0:T(8,128)} %convert_reduce_fusion) | data formatting | bytes 1572864 | tf_op jit(solution)/shard_map/reshape | solution.py:162
  174.6 2.2 %fusion.13 = bf16[8,2048]{1,0:T(8,128)(2,1)} fusion(f32[8,96]{1,0:T(8,128)S(1)} %select_reduce_fusion, f32[96,2048]{1,0:T(8,128)} %reshape.223, bf16[8,2048]{1,0:T(8,128)(2,1)S(1)} %copy-done.1, pred[8]{0:T(512)(128)(4,1)S(1)} %dynamic-slice_bitcast_fusion, bf16[32,2048]{1,0:T(8,128)(2,1)S(1)} %all_gather.15, s32[]{:T(128)S(6)} %select_n.34), kind=kOutput, calls=%fused_computation.15 | convolution fusion | flops 18972672 | bytes 887820 | tf_op jit(solution)/shard_map/dot_general | solution.py:165
  (25 shorter events, 0.2 us)
Async XLA Ops:
  7.2 125.7 %copy-start = (bf16[1,704,2048]{2,1,0:T(8,128)(2,1)S(1)}, bf16[1,704,2048]{2,1,0:T(8,128)(2,1)}, u32[]{:S(2)}) copy-start(bf16[1,704,2048]{2,1,0:T(8,128)(2,1)} %param.25) | copy-start | bytes 8650756
  7.2 39.7 %copy-start.8 = (u32[32]{0:T(128)S(1)}, u32[32]{0:T(128)}, u32[]{:S(2)}) copy-start(u32[32]{0:T(128)} %constant.82) | copy-start | bytes 388
  7.2 38.7 %copy-start.4 = (s32[8,6]{1,0:T(8,128)S(1)}, s32[8,6]{1,0:T(8,128)}, u32[]{:S(2)}) copy-start(s32[8,6]{1,0:T(8,128)} %param.21) | copy-start | bytes 580
  7.2 38.8 %copy-start.7 = (s32[16]{0:T(128)S(1)}, s32[16]{0:T(128)}, u32[]{:S(2)}) copy-start(s32[16]{0:T(128)} %param.23) | copy-start | bytes 196
  7.2 53.3 %copy-start.6 = (f32[512]{0:T(512)S(1)}, f32[512]{0:T(512)}, u32[]{:S(2)}) copy-start(f32[512]{0:T(512)} %param.18) | copy-start | bytes 6148
  7.2 64.4 %all-gather.3.cloned.1.call-start = ((), (), s32[]{:S(2)}) async-start(), calls=%async_computation.3 | async-start | bytes 4718592 | tf_op jit(solution)/shard_map/all_gather | solution.py:114
  8.0 87.1 %reduce-scatter.2.cloned.1.call-start = ((), (), s32[]{:S(2)}) async-start(), calls=%async_computation.4 | async-start | bytes 163840 | tf_op jit(solution)/shard_map/reduce_scatter | solution.py:117
  45.0 50.9 %copy-start.3 = (f32[2048]{0:T(1024)S(1)}, f32[2048]{0:T(1024)}, u32[]{:S(2)}) copy-start(f32[2048]{0:T(1024)} %param.20) | copy-start | bytes 24580
  60.7 9.6 %copy-start.2 = (bf16[32,576]{1,0:T(8,128)(2,1)}, bf16[32,576]{1,0:T(8,128)(2,1)S(1)}, u32[]{:S(2)}) copy-start(bf16[32,576]{1,0:T(8,128)(2,1)S(1)} %pad_maximum_fusion) | copy-start | bytes 110596
  132.9 11.9 %copy-start.5 = (f32[8,6]{1,0:T(8,128)S(1)}, f32[8,6]{1,0:T(8,128)}, u32[]{:S(2)}) copy-start(f32[8,6]{1,0:T(8,128)} %param.22) | copy-start | bytes 580
  137.9 36.7 %copy-start.1 = (bf16[8,2048]{1,0:T(8,128)(2,1)S(1)}, bf16[8,2048]{1,0:T(8,128)(2,1)}, u32[]{:S(2)}) copy-start(bf16[8,2048]{1,0:T(8,128)(2,1)} %reduce-scatter.2.cloned.1.call-done) | copy-start | bytes 98308
  140.2 29.6 %all-to-all-start.1 = ((bf16[32,6,2048]{2,1,0:T(8,128)(2,1)}), bf16[32,6,2048]{2,1,0:T(8,128)(2,1)}, u32[]{:S(2)}, u32[]{:S(2)}) async-start(bf16[32,6,2048]{2,1,0:T(8,128)(2,1)} %reshape.222), calls=%async_computation.2 | async-start | bytes 2097152 | tf_op jit(solution)/shard_map/all_to_all | solution.py:156
Sparse Core Ops, SparseCore 0:
  9.9 40.1 all-gather.2
  75.6 19.3 reduce-scatter.1
where the time goes:
time: 186 us; the launch traced here: 184 us
  blocking collectives  77.6 us (42%)
  waiting for transfers between devices  45 us (24%)
  matrix products  22.8 us (12%)
  between operations  14.9 us (8%)
  local copies, waits for them, and re-layouts  12.1 us (7%)
  other arithmetic  6.6 us (4%)
  starting transfers between devices  4.67 us (3%)
    all_to_all x1, blocking collectives, per_device(): lax.all_to_all(copies, ('context', 'span'), split_axis=0, concat_axis=0,...  27.8 us
    all_to_all x1, waiting for transfers between devices, per_device(): lax.all_to_all(partial_rows, ('context', 'span'), split_axis=0, concat_ax...  24.8 us
    reduce_scatter x1, waiting for transfers between devices, per_device(): lax.psum_scatter(jnp.einsum('hqd,hdm->qm', mixed, head_weights, preferred...  19.5 us
    all_gather x1, blocking collectives, per_device(): compact = lax.all_gather(picked, 'span', axis=1, tiled=True)  15.1 us
    all_gather x1, blocking collectives, per_device(): latent = lax.all_gather(latent_part, 'span', axis=1, tiled=True)  13.6 us
    unnamed x1, blocking collectives  11.8 us
    all_gather x1, blocking collectives, per_device(): key_rows = lax.all_gather(cached, 'context', axis=0, tiled=True)  9.34 us
    dot_general x1, matrix products, piece_work(): jnp.dot(hidden, expert_out[0], preferred_element_type=jnp.float32)  5.03 us
  transfers between devices with their start and end apart: 3, of which 2 were waited for; matrix products, arithmetic and copies ran while one was open for 7% of the time, Pallas kernels for 0%

commit v1 on v0

v1 whole, which is shorter than its diff:
```python
import functools

import jax
import jax.numpy as jnp
from jax import lax
from jax.experimental import pallas as pl
from jax.experimental.pallas import tpu as pltpu
from jax.sharding import PartitionSpec as P

EPS = 1e-06
THETA = 50000.0
SCALE = 192.0 ** (-0.5)
NEGATIVE = -1e30
F32 = jnp.float32
BF16 = jnp.bfloat16


def xor(value, bits):
    out = value
    bit = 1
    while bit <= bits:
        if bits & bit:
            out = out + bit * (1 - 2 * ((value // bit) % 2))
        bit *= 2
    return out


def rotate(values, cosine, sine):
    half = values.shape[-1] // 2
    swapped = jnp.concatenate([values[:, half:], values[:, :half]], axis=1)
    return values * cosine + swapped * sine


def normalized(values, gain):
    factor = lax.rsqrt(jnp.mean(values * values, axis=-1, keepdims=True) + EPS)
    return values * factor * gain


def dot(a, b):
    return jnp.dot(a, b, preferred_element_type=F32)


def kernel(
    n,
    spans,
    raw,
    keep,
    cosine,
    sine,
    attn_gain,
    kv_gain,
    moe_gain,
    ids,
    gate_values,
    slot_col,
    query_hbm,
    latent_hbm,
    out_hbm,
    in_hbm,
    down_hbm,
    layer_out,
    cache_out,
    query_w,
    latent_w,
    out_w,
    in_w,
    down_w,
    picked,
    normed,
    query_acc,
    latents,
    keys,
    mixed,
    part_send,
    part_recv,
    att_send,
    att_recv,
    folded,
    moe_rows,
    gate_acc,
    up_acc,
    pair_send,
    pair_recv,
    own_sum,
    plane_send,
    plane_recv,
    last_send,
    last_recv,
    load_sem,
    z_send,
    z_recv,
    p_send,
    p_recv,
    pair_sem,
):
    c = lax.axis_index("context")
    s = lax.axis_index("span")
    core = c % 2
    half_n = n // 2
    keep_count = keep.shape[0]
    rows_dev = layer_out.shape[0]
    model_width = layer_out.shape[1]
    latent_width = cache_out.shape[1]
    kv_rank = kv_gain.shape[1]
    heads = query_w.shape[1] // latent_width
    experts = slot_col.shape[0]
    raw_rows = raw.shape[0]

    def slot(ctx):
        return (ctx % 2) * half_n + ctx // 2

    sources = (query_hbm, latent_hbm, out_hbm, in_hbm, down_hbm)
    targets = (query_w, latent_w, out_w, in_w, down_w)
    loads = [
        pltpu.make_async_copy(a, b, load_sem.at[i])
        for i, (a, b) in enumerate(zip(sources, targets))
    ]
    for i in (1, 0, 2, 3, 4):
        loads[i].start()

    barrier = pltpu.get_barrier_semaphore()
    for k in range(1, n):
        pl.semaphore_signal(
            barrier, 1, device_id={"context": xor(c, k)}, device_id_type=pl.DeviceIdType.MESH
        )
    for k in range(1, spans):
        pl.semaphore_signal(
            barrier, 1, device_id={"span": xor(s, k)}, device_id_type=pl.DeviceIdType.MESH
        )

    def remote(src, dst, axis, peer, send, recv):
        return pltpu.make_async_remote_copy(
            src_ref=src,
            dst_ref=dst,
            send_sem=send,
            recv_sem=recv,
            device_id={axis: peer},
            device_id_type=pl.DeviceIdType.MESH,
        )

    pending = []

    def push(*args):
        copy = remote(*args)
        copy.start()
        pending.append(copy)

    def z_gather_start(buf, phase):
        for k in range(1, spans):
            push(
                buf.at[s], buf.at[s], "span", xor(s, k), z_send.at[phase, k], z_recv.at[phase, k]
            )

    def z_gather_wait(buf, phase):
        for k in range(1, spans):
            peer = xor(s, k)
            remote(
                buf.at[s], buf.at[peer], "span", peer, z_send.at[phase, k], z_recv.at[phase, k]
            ).wait_recv()

    def z_scatter(send_buf, recv_buf, phase):
        for k in range(1, spans):
            peer = xor(s, k)
            push(
                send_buf.at[peer],
                recv_buf.at[s],
                "span",
                peer,
                z_send.at[phase, k],
                z_recv.at[phase, k],
            )

    def z_scatter_sum(send_buf, recv_buf, phase):
        total = send_buf[s].astype(F32)
        for k in range(1, spans):
            peer = xor(s, k)
            remote(
                send_buf.at[peer],
                recv_buf.at[peer],
                "span",
                peer,
                z_send.at[phase, k],
                z_recv.at[phase, k],
            ).wait_recv()
            total = total + recv_buf[peer].astype(F32)
        return total

    def p_block(buf, phase, k, peer, block):
        return (
            buf.at[slot(block)],
            buf.at[slot(block)],
            "context",
            peer,
            p_send.at[phase, k],
            p_recv.at[phase, k],
        )

    def p_gather_start(buf, phase):
        for k in range(n - 1, 0, -2):
            push(*p_block(buf, phase, k, xor(c, k), c))

    def p_gather_forward(buf, phase):
        for k in range(1, n, 2):
            block = xor(c, k)
            remote(*p_block(buf, phase, k, block, block)).wait_recv()
            if k > 1:
                push(*p_block(buf, phase, k - 1, xor(c, 1), block))

    def p_gather_finish(buf, phase):
        for k in range(2, n, 2):
            block = xor(c, k)
            remote(*p_block(buf, phase, k, block, block)).wait_recv()

    listing = keep[...]
    live = listing >= 0
    chosen = lax.broadcasted_iota(jnp.int32, (keep_count, raw_rows), 1) == listing
    picked[s] = dot(chosen.astype(F32).astype(BF16), raw[...]).astype(BF16)

    pl.semaphore_wait(barrier, n - 1 + spans - 1)
    z_gather_start(picked, 0)
    hits = jnp.zeros((rows_dev, experts), F32)
    expert_lane = lax.broadcasted_iota(jnp.int32, (rows_dev, experts), 1)
    for t in range(ids.shape[1]):
        hits = hits + jnp.where(ids[:, t : t + 1] == expert_lane, gate_values[:, t : t + 1], 0.0)
    hits_high = hits.astype(BF16)
    hits_low = (hits - hits_high.astype(F32)).astype(BF16)
    lane = lax.broadcasted_iota(jnp.int32, (experts, 128), 1)
    place_high = (lane == slot_col[...]).astype(F32).astype(BF16)
    place_low = (lane == slot_col[...] + 64).astype(F32).astype(BF16)
    gate_lanes = dot(hits_high, place_high) + dot(hits_low, place_low)
    z_gather_wait(picked, 0)
    compact = jnp.concatenate([picked[i] for i in range(spans)], axis=1).astype(F32)
    normed[...] = normalized(compact, attn_gain[...]).astype(BF16)
    own_rows = jnp.zeros((rows_dev, model_width), F32)
    own_keep = jnp.zeros((rows_dev, 1), jnp.int32)
    for i in range(spans):
        own_rows = jnp.where(s == i, compact[i * rows_dev : (i + 1) * rows_dev], own_rows)
        own_keep = jnp.where(s == i, listing[i * rows_dev : (i + 1) * rows_dev], own_keep)

    loads[1].wait()
    latents[s] = dot(normed[...], latent_w[...])
    z_gather_start(latents, 1)
    loads[0].wait()
    query_acc[...] = jnp.zeros_like(query_acc)
    depth = 512

    def query_step(i, _):
        cut = pl.ds(pl.multiple_of(i * depth, depth), depth)
        query_acc[...] += dot(normed[:, cut], query_w[cut, :])
        return 0

    lax.fori_loop(0, model_width // depth, query_step, 0)
    z_gather_wait(latents, 1)
    latent = jnp.concatenate([latents[i] for i in range(spans)], axis=1)
    cos2, sin2 = cosine[...], sine[...]
    pad = -latent_width % 128
    flags = jnp.where(
        (lax.broadcasted_iota(jnp.int32, (keep_count, pad), 1) == 0) & live, 1.0, 0.0
    )
    tail = jnp.concatenate([rotate(latent[:, kv_rank:], cos2, sin2), flags], axis=1)
    block = jnp.concatenate([normalized(latent[:, :kv_rank], kv_gain[...]), tail], axis=1)
    block = block.astype(BF16)
    keys[slot(c)] = block
    p_gather_start(keys, 0)
    cache_out[...] = block[:, :latent_width]
    parts = []
    for h in range(heads):
        q = query_acc[:, h * latent_width : (h + 1) * latent_width]
        parts.append(
            jnp.concatenate(
                [
                    q[:, :kv_rank],
                    rotate(q[:, kv_rank:], cos2, sin2),
                    jnp.zeros((keep_count, pad), F32),
                ],
                axis=1,
            )
        )
    query = jnp.concatenate(parts, axis=0).astype(BF16)
    tokens = n * keep_count
    rows = heads * keep_count
    key_lane = lax.broadcasted_iota(jnp.int32, (rows, tokens), 1)
    query_row = lax.broadcasted_iota(jnp.int32, (rows, tokens), 0) & (keep_count - 1)
    shift = keep_count.bit_length() - 1
    key_slot = lax.shift_right_logical(key_lane, shift)
    key_ctx = (key_slot & (half_n - 1)) * 2 + lax.shift_right_logical(
        key_slot, half_n.bit_length() - 1
    )
    causal = key_ctx * keep_count + (key_lane & (keep_count - 1)) <= query_row + c * keep_count
    pick_flag = jnp.where(
        lax.broadcasted_iota(jnp.int32, (16, latent_width + pad), 1) == latent_width, 1.0, 0.0
    ).astype(BF16)
    p_gather_forward(keys, 0)
    p_gather_finish(keys, 0)
    all_keys = keys[...].reshape(tokens, latent_width + pad)
    contract = (((1,), (1,)), ((), ()))
    scores = lax.dot_general(query, all_keys, contract, preferred_element_type=F32) * SCALE
    key_live = lax.dot_general(pick_flag, all_keys, contract, preferred_element_type=F32)[:1]
    allowed = causal & (key_live > 0)
    scores = jnp.where(allowed, scores, NEGATIVE)
    highest = jnp.max(scores, axis=1, keepdims=True)
    weights = jnp.where(allowed, jnp.exp(scores - highest), 0.0)
    denominator = jnp.sum(weights, axis=1, keepdims=True)
    summed = dot(weights.astype(BF16), all_keys[:, :kv_rank]) / denominator
    mixed[slot(c)] = jnp.concatenate(
        [summed[h * keep_count : (h + 1) * keep_count] for h in range(heads)], axis=1
    ).astype(BF16)
    p_gather_start(mixed, 1)
    loads[2].wait()
    p_gather_forward(mixed, 1)
    p_gather_finish(mixed, 1)
    columns = out_w.shape[1]
    projected = dot(mixed[...].reshape(tokens, heads * kv_rank), out_w[...])
    projected = projected.reshape(n, spans, rows_dev, columns)
    for i in range(spans):
        part_send[i] = projected[:, i].reshape(n * rows_dev, columns).astype(BF16)
    z_scatter(part_send, part_recv, 2)
    attended = z_scatter_sum(part_send, part_recv, 2)
    for i in range(n):
        att_send[i] = attended[i * rows_dev : (i + 1) * rows_dev]
    for k in range(n - 1, 0, -1):
        peer = xor(c, k)
        push(
            att_send.at[slot(peer)],
            att_recv.at[c],
            "context",
            peer,
            p_send.at[2, k],
            p_recv.at[2, k],
        )
    att_recv[c] = att_send[slot(c)]
    for k in range(1, n):
        peer = xor(c, k)
        remote(
            att_send.at[slot(peer)],
            att_recv.at[peer],
            "context",
            peer,
            p_send.at[2, k],
            p_recv.at[2, k],
        ).wait_recv()
    resid = own_rows + jnp.concatenate([att_recv[i] for i in range(n)], axis=1)
    moe_in = normalized(resid, moe_gain[...])
    half_width = folded.shape[2]
    wide = jnp.concatenate(
        [moe_in, gate_lanes, jnp.zeros((rows_dev, 2 * half_width - model_width - 128), F32)],
        axis=1,
    )
    folded[s] = jnp.concatenate([wide[:, :half_width], wide[:, half_width:]], axis=0).astype(BF16)
    z_gather_start(folded, 3)
    z_gather_wait(folded, 3)
    blocks = []
    for i in range(spans):
        v = folded[i].astype(F32)
        blocks.append(
            jnp.concatenate([v[:rows_dev], v[rows_dev:]], axis=1)[:, : model_width + 128]
        )
    moe_rows[slot(c)] = jnp.concatenate(blocks, axis=0).astype(BF16)
    p_gather_start(moe_rows, 3)

    stored = (c * spans + s) // 2
    many = half_n * keep_count
    width = 512

    def expert(base, target):
        lanes = lax.broadcasted_iota(jnp.int32, (many, 128), 1)
        gate_block = moe_rows[pl.ds(base, half_n), :, model_width:].reshape(many, 128)
        scale = jnp.sum(
            jnp.where(
                (lanes == stored) | (lanes == stored + 64), gate_block.astype(F32), 0.0
            ),
            axis=1,
            keepdims=True,
        )
        gate_acc[...] = jnp.zeros_like(gate_acc)
        up_acc[...] = jnp.zeros_like(up_acc)

        def step(i, _):
            cut = pl.ds(pl.multiple_of(i * depth, depth), depth)
            x = moe_rows[pl.ds(base, half_n), :, cut].reshape(many, depth)
            gate_acc[...] += dot(x, in_w[0, 0, cut, :])
            up_acc[...] += dot(x, in_w[0, 1, cut, :])
            return 0

        lax.fori_loop(0, model_width // depth, step, 0)
        gate = gate_acc[...]
        hidden = (gate / (1.0 + jnp.exp(-gate)) * up_acc[...]).astype(BF16)

        def down(i, _):
            cut = pl.ds(pl.multiple_of(i * width, width), width)
            made = dot(hidden, down_w[0, :, cut]) * scale
            target[:, :, cut] = made.reshape(half_n, keep_count, width).astype(BF16)
            return 0

        lax.fori_loop(0, model_width // width, down, 0)

    p_gather_forward(moe_rows, 3)
    loads[3].wait()
    loads[4].wait()
    expert((1 - core) * half_n, pair_send)
    pair = (pair_send, pair_recv, "context", xor(c, 1), pair_sem.at[0], pair_sem.at[1])
    push(*pair)
    p_gather_finish(moe_rows, 3)
    expert(core * half_n, own_sum)
    remote(*pair).wait_recv()
    for k in range(n - 2, 0, -2):
        peer = xor(c, k)
        chip = peer // 2
        plane_send[chip] = (own_sum[chip].astype(F32) + pair_recv[chip].astype(F32)).astype(BF16)
        push(
            plane_send.at[chip],
            plane_recv.at[c // 2],
            "context",
            peer,
            p_send.at[4, k],
            p_recv.at[4, k],
        )
    total = own_sum[c // 2].astype(F32) + pair_recv[c // 2].astype(F32)
    for k in range(2, n, 2):
        peer = xor(c, k)
        chip = peer // 2
        remote(
            plane_send.at[chip],
            plane_recv.at[chip],
            "context",
            peer,
            p_send.at[4, k],
            p_recv.at[4, k],
        ).wait_recv()
        total = total + plane_recv[chip].astype(F32)
    middle = model_width // 2
    for i in range(spans):
        v = total[i * rows_dev : (i + 1) * rows_dev]
        last_send[i] = jnp.concatenate([v[:, :middle], v[:, middle:]], axis=0).astype(BF16)
    z_scatter(last_send, last_recv, 4)
    routed = z_scatter_sum(last_send, last_recv, 4)
    routed = jnp.concatenate([routed[:rows_dev], routed[rows_dev:]], axis=1)
    layer_out[...] = jnp.where(own_keep >= 0, resid + routed, 0.0).astype(BF16)
    for copy in pending:
        copy.wait_send()


def per_device(
    raw_tokens,
    keep,
    attn_gain,
    query_weight,
    latent_weight,
    kv_gain,
    out_weight,
    moe_gain,
    expert_ids,
    gate_values,
    expert_slot,
    expert_in,
    expert_out,
):
    n = lax.axis_size("context")
    spans = lax.axis_size("span")
    kv_rank = kv_gain.shape[0]
    local_latent = latent_weight.shape[1]
    latent_width = local_latent * spans
    model_width = attn_gain.shape[0]
    keep_count = keep.shape[1]
    raw_rows = raw_tokens.shape[0]
    rows_dev = expert_ids.shape[0]
    rotary_width = latent_width - kv_rank
    half = rotary_width // 2
    key_width = latent_width + (-latent_width % 128)
    many = n // 2 * keep_count
    hidden = expert_in.shape[3]
    columns = out_weight.shape[1]
    mixed_width = out_weight.shape[0]
    wide = model_width + 128
    half_width = (wide + 255) // 256 * 128
    listing = keep[0]
    positions = lax.axis_index("context") * raw_rows + jnp.maximum(listing, 0)
    freqs = THETA ** (-2.0 * jnp.arange(half, dtype=F32) / rotary_width)
    angles = positions.astype(F32)[:, None] * freqs[None, :]
    cosine, sine = jnp.cos(angles), jnp.sin(angles)
    cos2 = jnp.concatenate([cosine, cosine], axis=1)
    sin2 = jnp.concatenate([-sine, sine], axis=1)
    vmem = pl.BlockSpec(memory_space=pltpu.VMEM)
    hbm = pl.BlockSpec(memory_space=pl.ANY)
    chips = n // 2
    return pl.pallas_call(
        functools.partial(kernel, n, spans),
        out_shape=(
            jax.ShapeDtypeStruct((rows_dev, model_width), BF16),
            jax.ShapeDtypeStruct((keep_count, latent_width), BF16),
        ),
        in_specs=[vmem] * 10 + [hbm] * 5,
        out_specs=(vmem, vmem),
        scratch_shapes=[
            pltpu.VMEM(query_weight.shape, BF16),
            pltpu.VMEM(latent_weight.shape, BF16),
            pltpu.VMEM(out_weight.shape, BF16),
            pltpu.VMEM(expert_in.shape, BF16),
            pltpu.VMEM(expert_out.shape, BF16),
            pltpu.VMEM((spans, keep_count, raw_tokens.shape[1]), BF16),
            pltpu.VMEM((keep_count, model_width), BF16),
            pltpu.VMEM((keep_count, query_weight.shape[1]), F32),
            pltpu.VMEM((spans, keep_count, local_latent), F32),
            pltpu.VMEM((n, keep_count, key_width), BF16),
            pltpu.VMEM((n, keep_count, mixed_width), BF16),
            pltpu.VMEM((spans, n * rows_dev, columns), BF16),
            pltpu.VMEM((spans, n * rows_dev, columns), BF16),
            pltpu.VMEM((n, rows_dev, columns), F32),
            pltpu.VMEM((n, rows_dev, columns), F32),
            pltpu.VMEM((spans, 2 * rows_dev, half_width), BF16),
            pltpu.VMEM((n, keep_count, wide), BF16),
            pltpu.VMEM((many, hidden), F32),
            pltpu.VMEM((many, hidden), F32),
            pltpu.VMEM((chips, keep_count, model_width), BF16),
            pltpu.VMEM((chips, keep_count, model_width), BF16),
            pltpu.VMEM((chips, keep_count, model_width), BF16),
            pltpu.VMEM((chips, keep_count, model_width), BF16),
            pltpu.VMEM((chips, keep_count, model_width), BF16),
            pltpu.VMEM((spans, 2 * rows_dev, model_width // 2), BF16),
            pltpu.VMEM((spans, 2 * rows_dev, model_width // 2), BF16),
            pltpu.SemaphoreType.DMA((5,)),
            pltpu.SemaphoreType.DMA((5, spans)),
            pltpu.SemaphoreType.DMA((5, spans)),
            pltpu.SemaphoreType.DMA((5, n)),
            pltpu.SemaphoreType.DMA((5, n)),
            pltpu.SemaphoreType.DMA((2,)),
        ],
        compiler_params=pltpu.CompilerParams(
            collective_id=0, has_side_effects=True, vmem_limit_bytes=56 * 1024 * 1024
        ),
    )(
        raw_tokens,
        listing[:, None],
        cos2,
        sin2,
        attn_gain[None, :],
        kv_gain[None, :],
        moe_gain[None, :],
        expert_ids,
        gate_values,
        expert_slot[:, None],
        query_weight,
        latent_weight,
        out_weight,
        expert_in,
        expert_out,
    )


def solution(mesh):
    placed = (
        P(("groups", "context"), "span"),
        P(("groups", "context"), None),
        P(),
        P(None, "span"),
        P(None, "span"),
        P(),
        P("span", "context"),
        P(),
        P(("groups", "context", "span"), None),
        P(("groups", "context", "span"), None),
        P(),
        P(("context", "span"), None, None, None),
        P(("context", "span"), None, None),
    )
    return jax.shard_map(
        per_device,
        mesh=mesh,
        in_specs=placed,
        out_specs=(P(("groups", "context", "span"), None), P(("groups", "context"), None)),
        check_vma=False,
    )
```

time: 186 us -> 84.9 us (0.46)
  blocking collectives: 77.6 us -> 0 us
  Pallas kernels: 0 us -> 66.1 us
  waiting for transfers between devices: 45 us -> 0 us
  matrix products: 22.8 us -> 0 us
  between operations: 14.9 us -> 0.65 us
  other arithmetic: 6.6 us -> 1.5 us
  starting transfers between devices: 4.67 us -> 0 us
  local copies, waits for them, and re-layouts: 12.1 us -> 16.2 us
    pallas_call x0 -> x1, Pallas kernels: none -> 66.1 us  [per_device(): pl.pallas_call(functools.partial(kernel, n, spans), out_shape=(jax.ShapeD...]
    all_gather x3 -> x0, blocking collectives: 38 us -> none  [the longest x1 15.1 us: per_device(): compact = lax.all_gather(picked, 'span', axis=1, tiled=True)]
    all_to_all x1 -> x0, blocking collectives: 27.8 us -> none  [per_device(): lax.all_to_all(copies, ('context', 'span'), split_axis=0, concat_axis=0,...]
    all_to_all x1 -> x0, waiting for transfers between devices: 24.8 us -> none  [per_device(): lax.all_to_all(partial_rows, ('context', 'span'), split_axis=0, concat_ax...]
    dot_general x8 -> x0, matrix products: 22.8 us -> none  [the longest x1 5.03 us: piece_work(): jnp.dot(hidden, expert_out[0], preferred_element_type=jnp.float32)]
    reduce_scatter x1 -> x0, waiting for transfers between devices: 19.5 us -> none  [per_device(): lax.psum_scatter(jnp.einsum('hqd,hdm->qm', mixed, head_weights, preferred...]
    unnamed x1 -> x0, blocking collectives: 11.8 us -> none
    unnamed x25 -> x4, local copies, waits for them, and re-layouts: 1.83 us -> 13.5 us
  transfers between devices with their start and end apart: 3 -> 0, of which waited for: 2 -> 0; matrix products, arithmetic and copies ran while one was open for 7% -> 0% of each run, Pallas kernels for 0% -> 0%
where the time goes in v1:
time: 84.9 us; the launch traced here: 84.4 us
  Pallas kernels  66.1 us (78%)
  local copies, waits for them, and re-layouts  16.2 us (19%)
  other arithmetic  1.5 us (2%)
    pallas_call x1, Pallas kernels, per_device(): pl.pallas_call(functools.partial(kernel, n, spans), out_shape=(jax.ShapeD...  66.1 us
    unnamed x4, local copies, waits for them, and re-layouts  13.5 us

profile of v1, /device:TPU:0, one launch (start us, length us, event | category | flops | bytes accessed | tf_op | source)
XLA Modules:
  0.0 84.4 jit_solution(10635477065405055358)
XLA Ops:
  0.6 0.7 convert_bitcast_fusion
  1.3 1.3 %copy.16.slot_col = s32[16,1]{1,0:T(8,128)} copy(s32[16,1]{0,1:T(1,128)} %bitcast.10) | data formatting | bytes 128 | tf_op jit(solution)/shard_map/broadcast_in_dim | solution.py:541
  2.6 1.3 %copy.15.keep = s32[32,1]{1,0:T(8,128)} copy(s32[32,1]{0,1:T(1,128)} %bitcast.11) | data formatting | bytes 256 | tf_op jit(solution)/shard_map/broadcast_in_dim;squeeze | solution.py:533
  4.0 0.1 fusion
  4.1 0.7 pad_maximum_fusion
  4.8 2.2 %copy.17.latent_hbm = bf16[2048,144]{1,0:T(8,128)(2,1)} copy(bf16[2048,144]{0,1:T(8,128)(2,1)} %param.17) | data formatting | bytes 1179648 | tf_op args[4]
  7.0 8.5 %copy.18.in_hbm = bf16[1,2,2048,704]{3,2,1,0:T(8,128)(2,1)} copy(bf16[1,2,2048,704]{2,3,1,0:T(8,128)(2,1)} %param.24) | data formatting | bytes 11534336 | tf_op args[11]
  15.5 66.1 %shard_map.140 = (bf16[8,2048]{1,0:T(8,128)(2,1)}, bf16[32,576]{1,0:T(8,128)(2,1)}) custom-call(bf16[192,512]{1,0:T(8,128)(2,1)} %raw.1, s32[32,1]{1,0:T(8,128)} %copy.15.keep, f32[32,64]{1,0:T(8,128)} %get-tuple-element.5.cosine, f32[32,64]{1,0:T(8,128)} %get-tuple-element.6.sine, f32[1,2048]{1,0:T(1,128)} %bitcast.7, f32[1,512]{1,0:T(1,128)} %bitcast.9, ...), custom_call_target="tpu_custom_call" | custom-call | tf_op jit(solution)/shard_map/pallas_call | solution.py:486
  81.6 1.4 %copy.21 = bf16[8,2048]{1,0:T(8,128)(2,1)} copy(bf16[8,2048]{1,0:T(8,128)(2,1)} %get-tuple-element.9) | data formatting | bytes 65536
  83.0 1.4 %copy.22 = bf16[32,576]{1,0:T(8,128)(2,1)} copy(bf16[32,576]{1,0:T(8,128)(2,1)} %get-tuple-element.10) | data formatting | bytes 73728
  (1 shorter events, 0.0 us)

commit v2 on v1

--- a/solution.py
+++ b/solution.py
@@ -2,6 +2,7 @@
 
 import jax
 import jax.numpy as jnp
+import numpy as np
 from jax import lax
 from jax.experimental import pallas as pl
 from jax.experimental.pallas import tpu as pltpu
@@ -40,19 +41,30 @@
     return jnp.dot(a, b, preferred_element_type=F32)
 
 
+def dot_rows(a, b):
+    return lax.dot_general(a, b, (((1,), (1,)), ((), ())), preferred_element_type=F32)
+
+
+def column(row):
+    size = row.shape[1]
+    same = lax.broadcasted_iota(jnp.int32, (size, size), 0) == lax.broadcasted_iota(
+        jnp.int32, (size, size), 1
+    )
+    return jnp.sum(jnp.where(same, row.astype(F32), 0.0), axis=1, keepdims=True).astype(jnp.int32)
+
+
 def kernel(
     n,
     spans,
     raw,
     keep,
-    cosine,
-    sine,
+    freqs,
     attn_gain,
     kv_gain,
     moe_gain,
     ids,
     gate_values,
-    slot_col,
+    slots,
     query_hbm,
     latent_hbm,
     out_hbm,
@@ -97,13 +109,13 @@
     s = lax.axis_index("span")
     core = c % 2
     half_n = n // 2
-    keep_count = keep.shape[0]
+    keep_count = keep.shape[1]
     rows_dev = layer_out.shape[0]
     model_width = layer_out.shape[1]
     latent_width = cache_out.shape[1]
     kv_rank = kv_gain.shape[1]
     heads = query_w.shape[1] // latent_width
-    experts = slot_col.shape[0]
+    experts = slots.shape[1]
     raw_rows = raw.shape[0]
 
     def slot(ctx):
@@ -211,7 +223,7 @@
             block = xor(c, k)
             remote(*p_block(buf, phase, k, block, block)).wait_recv()
 
-    listing = keep[...]
+    listing = column(keep[...])
     live = listing >= 0
     chosen = lax.broadcasted_iota(jnp.int32, (keep_count, raw_rows), 1) == listing
     picked[s] = dot(chosen.astype(F32).astype(BF16), raw[...]).astype(BF16)
@@ -225,9 +237,16 @@
     hits_high = hits.astype(BF16)
     hits_low = (hits - hits_high.astype(F32)).astype(BF16)
     lane = lax.broadcasted_iota(jnp.int32, (experts, 128), 1)
-    place_high = (lane == slot_col[...]).astype(F32).astype(BF16)
-    place_low = (lane == slot_col[...] + 64).astype(F32).astype(BF16)
+    slot_col = column(slots[...])
+    place_high = (lane == slot_col).astype(F32).astype(BF16)
+    place_low = (lane == slot_col + 64).astype(F32).astype(BF16)
     gate_lanes = dot(hits_high, place_high) + dot(hits_low, place_low)
+    positions = (c * raw_rows + jnp.maximum(listing, 0)).astype(F32)
+    angles = positions * freqs[...]
+    cos2 = jnp.cos(angles)
+    rotary = freqs.shape[1]
+    first = lax.broadcasted_iota(jnp.int32, (keep_count, rotary), 1) < rotary // 2
+    sin2 = jnp.where(first, -1.0, 1.0) * jnp.sin(angles)
     z_gather_wait(picked, 0)
     compact = jnp.concatenate([picked[i] for i in range(spans)], axis=1).astype(F32)
     normed[...] = normalized(compact, attn_gain[...]).astype(BF16)
@@ -238,7 +257,7 @@
         own_keep = jnp.where(s == i, listing[i * rows_dev : (i + 1) * rows_dev], own_keep)
 
     loads[1].wait()
-    latents[s] = dot(normed[...], latent_w[...])
+    latents[s] = dot_rows(normed[...], latent_w[...])
     z_gather_start(latents, 1)
     loads[0].wait()
     query_acc[...] = jnp.zeros_like(query_acc)
@@ -252,7 +271,6 @@
     lax.fori_loop(0, model_width // depth, query_step, 0)
     z_gather_wait(latents, 1)
     latent = jnp.concatenate([latents[i] for i in range(spans)], axis=1)
-    cos2, sin2 = cosine[...], sine[...]
     pad = -latent_width % 128
     flags = jnp.where(
         (lax.broadcasted_iota(jnp.int32, (keep_count, pad), 1) == 0) & live, 1.0, 0.0
@@ -293,9 +311,8 @@
     p_gather_forward(keys, 0)
     p_gather_finish(keys, 0)
     all_keys = keys[...].reshape(tokens, latent_width + pad)
-    contract = (((1,), (1,)), ((), ()))
-    scores = lax.dot_general(query, all_keys, contract, preferred_element_type=F32) * SCALE
-    key_live = lax.dot_general(pick_flag, all_keys, contract, preferred_element_type=F32)[:1]
+    scores = dot_rows(query, all_keys) * SCALE
+    key_live = dot_rows(pick_flag, all_keys)[:1]
     allowed = causal & (key_live > 0)
     scores = jnp.where(allowed, scores, NEGATIVE)
     highest = jnp.max(scores, axis=1, keepdims=True)
@@ -378,8 +395,8 @@
         def step(i, _):
             cut = pl.ds(pl.multiple_of(i * depth, depth), depth)
             x = moe_rows[pl.ds(base, half_n), :, cut].reshape(many, depth)
-            gate_acc[...] += dot(x, in_w[0, 0, cut, :])
-            up_acc[...] += dot(x, in_w[0, 1, cut, :])
+            gate_acc[...] += dot_rows(x, in_w[0, 0, :, cut])
+            up_acc[...] += dot_rows(x, in_w[0, 1, :, cut])
             return 0
 
         lax.fori_loop(0, model_width // depth, step, 0)
@@ -462,7 +479,6 @@
     latent_width = local_latent * spans
     model_width = attn_gain.shape[0]
     keep_count = keep.shape[1]
-    raw_rows = raw_tokens.shape[0]
     rows_dev = expert_ids.shape[0]
     rotary_width = latent_width - kv_rank
     half = rotary_width // 2
@@ -473,15 +489,12 @@
     mixed_width = out_weight.shape[0]
     wide = model_width + 128
     half_width = (wide + 255) // 256 * 128
-    listing = keep[0]
-    positions = lax.axis_index("context") * raw_rows + jnp.maximum(listing, 0)
-    freqs = THETA ** (-2.0 * jnp.arange(half, dtype=F32) / rotary_width)
-    angles = positions.astype(F32)[:, None] * freqs[None, :]
-    cosine, sine = jnp.cos(angles), jnp.sin(angles)
-    cos2 = jnp.concatenate([cosine, cosine], axis=1)
-    sin2 = jnp.concatenate([-sine, sine], axis=1)
+    latent_weight = latent_weight.T
+    expert_in = jnp.swapaxes(expert_in, 2, 3)
+    freqs = THETA ** (-2.0 * np.arange(half, dtype=np.float64) / rotary_width)
+    freqs = jnp.asarray(np.tile(freqs, 2)[None, :], F32)
     vmem = pl.BlockSpec(memory_space=pltpu.VMEM)
-    hbm = pl.BlockSpec(memory_space=pl.ANY)
+    hbm = pl.BlockSpec(memory_space=pltpu.HBM)
     chips = n // 2
     return pl.pallas_call(
         functools.partial(kernel, n, spans),
@@ -489,7 +502,7 @@
             jax.ShapeDtypeStruct((rows_dev, model_width), BF16),
             jax.ShapeDtypeStruct((keep_count, latent_width), BF16),
         ),
-        in_specs=[vmem] * 10 + [hbm] * 5,
+        in_specs=[vmem] * 9 + [hbm] * 5,
         out_specs=(vmem, vmem),
         scratch_shapes=[
             pltpu.VMEM(query_weight.shape, BF16),
@@ -526,19 +539,18 @@
             pltpu.SemaphoreType.DMA((2,)),
         ],
         compiler_params=pltpu.CompilerParams(
-            collective_id=0, has_side_effects=True, vmem_limit_bytes=56 * 1024 * 1024
+            collective_id=0, has_side_effects=True, vmem_limit_bytes=53 * 1024 * 1024
         ),
     )(
         raw_tokens,
-        listing[:, None],
-        cos2,
-        sin2,
+        keep,
+        freqs,
         attn_gain[None, :],
         kv_gain[None, :],
         moe_gain[None, :],
         expert_ids,
         gate_values,
-        expert_slot[:, None],
+        expert_slot[None, :],
         query_weight,
         latent_weight,
         out_weight,

time: 84.9 us -> 75.6 us (0.89)
  local copies, waits for them, and re-layouts: 16.2 us -> 8.61 us
  other arithmetic: 1.5 us -> 0 us
    unnamed x4 -> x22, local copies, waits for them, and re-layouts: 13.5 us -> 8.61 us
    another operation x1 -> x0, local copies, waits for them, and re-layouts: 1.34 us -> none  [per_device(): listing[:, None]]
    broadcast_in_dim x1 -> x0, local copies, waits for them, and re-layouts: 1.33 us -> none  [per_device(): expert_slot[:, None]]
where the time goes in v2:
time: 75.6 us; the launch traced here: 75.2 us
  Pallas kernels  65.9 us (87%)
  local copies, waits for them, and re-layouts  8.61 us (11%)
    pallas_call x1, Pallas kernels, per_device(): pl.pallas_call(functools.partial(kernel, n, spans), out_shape=(jax.ShapeD...  65.9 us
    unnamed x22, local copies, waits for them, and re-layouts  8.61 us

profile of v2, /device:TPU:0, one launch (start us, length us, event | category | flops | bytes accessed | tf_op | source)
XLA Modules:
  0.0 75.2 jit_solution(15197328230003003779)
XLA Ops:
  0.6 0.0 copy-start
  0.6 1.0 %copy-done = bf16[1024,256]{1,0:T(8,128)(2,1)S(1)} copy-done((bf16[1024,256]{1,0:T(8,128)(2,1)S(1)}, bf16[1024,256]{1,0:T(8,128)(2,1)}, u32[]{:S(2)}) %copy-start) | copy-done | bytes 524312
  1.7 0.0 copy-start.1
  1.7 0.9 %copy-done.1 = bf16[192,512]{1,0:T(8,128)(2,1)S(1)} copy-done((bf16[192,512]{1,0:T(8,128)(2,1)S(1)}, bf16[192,512]{1,0:T(8,128)(2,1)}, u32[]{:S(2)}) %copy-start.1) | copy-done | bytes 196632
  2.6 0.0 copy-start.2
  2.6 0.7 copy-done.2
  3.3 0.0 copy-start.3
  3.3 0.7 copy-done.3
  4.0 0.0 copy-start.4
  4.0 0.7 copy-done.4
  4.7 0.0 copy-start.5
  4.7 0.7 copy-done.5
  5.4 0.0 copy-start.6
  5.4 0.7 copy-done.6
  6.1 0.0 copy-start.7
  6.1 0.7 copy-done.7
  6.7 0.0 copy-start.8
  6.7 0.7 copy-done.8
  7.4 0.0 copy-start.9
  7.4 0.7 copy-done.9
  8.0 65.9 %shard_map.149 = (bf16[8,2048]{1,0:T(8,128)(2,1)S(1)}, bf16[32,576]{1,0:T(8,128)(2,1)S(1)}) custom-call(bf16[192,512]{1,0:T(8,128)(2,1)S(1)} %copy-done.1, s32[1,32]{1,0:T(1,128)S(1)} %copy-done.7, f32[1,64]{1,0:T(1,128)S(1)} %copy-done.9, f32[1,2048]{1,0:T(1,128)S(1)} %bitcast.6, f32[1,512]{1,0:T(1,128)S(1)} %bitcast.8, f32[1,2048]{1,0:T(1,128)S(1)} %bitcast.7, ...), custom_call_target="tpu_custom_call" | custom-call | tf_op jit(solution)/shard_map/pallas_call | solution.py:499
  74.0 0.6 copy.18
  74.6 0.6 copy.19
Async XLA Ops:
  0.6 1.0 %copy-start = (bf16[1024,256]{1,0:T(8,128)(2,1)S(1)}, bf16[1024,256]{1,0:T(8,128)(2,1)}, u32[]{:S(2)}) copy-start(bf16[1024,256]{1,0:T(8,128)(2,1)} %out_hbm.1) | copy-start | bytes 1572868
  1.7 0.9 %copy-start.1 = (bf16[192,512]{1,0:T(8,128)(2,1)S(1)}, bf16[192,512]{1,0:T(8,128)(2,1)}, u32[]{:S(2)}) copy-start(bf16[192,512]{1,0:T(8,128)(2,1)} %raw.1) | copy-start | bytes 589828
  2.6 0.7 copy-start.2
  3.3 0.7 copy-start.3
  4.0 0.7 copy-start.4
  4.7 0.7 copy-start.5
  5.4 0.7 copy-start.6
  6.1 0.7 copy-start.7
  6.7 0.7 copy-start.8
  7.4 0.7 copy-start.9

commit v3 on v2

--- a/solution.py
+++ b/solution.py
@@ -324,27 +324,32 @@
     ).astype(BF16)
     p_gather_start(mixed, 1)
     loads[2].wait()
-    p_gather_forward(mixed, 1)
-    p_gather_finish(mixed, 1)
     columns = out_w.shape[1]
-    projected = dot(mixed[...].reshape(tokens, heads * kv_rank), out_w[...])
-    projected = projected.reshape(n, spans, rows_dev, columns)
-    for i in range(spans):
-        part_send[i] = projected[:, i].reshape(n * rows_dev, columns).astype(BF16)
-    z_scatter(part_send, part_recv, 2)
-    attended = z_scatter_sum(part_send, part_recv, 2)
-    for i in range(n):
-        att_send[i] = attended[i * rows_dev : (i + 1) * rows_dev]
-    for k in range(n - 1, 0, -1):
-        peer = xor(c, k)
-        push(
-            att_send.at[slot(peer)],
-            att_recv.at[c],
-            "context",
-            peer,
-            p_send.at[2, k],
-            p_recv.at[2, k],
-        )
+    bases = ((1 - core) * half_n, core * half_n)
+    for turn in range(2):
+        if turn == 0:
+            p_gather_forward(mixed, 1)
+        else:
+            p_gather_finish(mixed, 1)
+        here = mixed[pl.ds(bases[turn], half_n)].reshape(half_n * keep_count, heads * kv_rank)
+        projected = dot(here, out_w[...]).reshape(half_n, spans, rows_dev, columns)
+        for i in range(spans):
+            part_send[turn, i] = projected[:, i].reshape(half_n * rows_dev, columns).astype(BF16)
+        z_scatter(part_send.at[turn], part_recv.at[turn], (2, 5)[turn])
+    for turn in range(2):
+        attended = z_scatter_sum(part_send.at[turn], part_recv.at[turn], (2, 5)[turn])
+        for i in range(half_n):
+            att_send[bases[turn] + i] = attended[i * rows_dev : (i + 1) * rows_dev]
+        for k in range(n - 1 - turn, 0, -2):
+            peer = xor(c, k)
+            push(
+                att_send.at[slot(peer)],
+                att_recv.at[c],
+                "context",
+                peer,
+                p_send.at[2, k],
+                p_recv.at[2, k],
+            )
     att_recv[c] = att_send[slot(c)]
     for k in range(1, n):
         peer = xor(c, k)
@@ -379,7 +384,7 @@
     many = half_n * keep_count
     width = 512
 
-    def expert(base, target):
+    def expert_up(base):
         lanes = lax.broadcasted_iota(jnp.int32, (many, 128), 1)
         gate_block = moe_rows[pl.ds(base, half_n), :, model_width:].reshape(many, 128)
         scale = jnp.sum(
@@ -403,55 +408,83 @@
         gate = gate_acc[...]
         hidden = (gate / (1.0 + jnp.exp(-gate)) * up_acc[...]).astype(BF16)
 
+        return hidden, scale
+
+    middle = model_width // 2
+
+    def expert_down(made_by, part, target):
+        hidden, scale = made_by
+
         def down(i, _):
             cut = pl.ds(pl.multiple_of(i * width, width), width)
-            made = dot(hidden, down_w[0, :, cut]) * scale
-            target[:, :, cut] = made.reshape(half_n, keep_count, width).astype(BF16)
+            source = pl.ds(pl.multiple_of(part * middle + i * width, width), width)
+            made = dot(hidden, down_w[0, :, source]) * scale
+            target[part, :, :, cut] = made.reshape(half_n, keep_count, width).astype(BF16)
             return 0
 
-        lax.fori_loop(0, model_width // width, down, 0)
+        lax.fori_loop(0, middle // width, down, 0)
+
+    def pair(part):
+        return (
+            pair_send.at[part],
+            pair_recv.at[part],
+            "context",
+            xor(c, 1),
+            pair_sem.at[0, part],
+            pair_sem.at[1, part],
+        )
 
     p_gather_forward(moe_rows, 3)
     loads[3].wait()
     loads[4].wait()
-    expert((1 - core) * half_n, pair_send)
-    pair = (pair_send, pair_recv, "context", xor(c, 1), pair_sem.at[0], pair_sem.at[1])
-    push(*pair)
+    made_by = expert_up(bases[0])
+    for part in range(2):
+        expert_down(made_by, part, pair_send)
+        push(*pair(part))
     p_gather_finish(moe_rows, 3)
-    expert(core * half_n, own_sum)
-    remote(*pair).wait_recv()
-    for k in range(n - 2, 0, -2):
-        peer = xor(c, k)
-        chip = peer // 2
-        plane_send[chip] = (own_sum[chip].astype(F32) + pair_recv[chip].astype(F32)).astype(BF16)
-        push(
-            plane_send.at[chip],
-            plane_recv.at[c // 2],
-            "context",
-            peer,
-            p_send.at[4, k],
-            p_recv.at[4, k],
-        )
-    total = own_sum[c // 2].astype(F32) + pair_recv[c // 2].astype(F32)
-    for k in range(2, n, 2):
-        peer = xor(c, k)
-        chip = peer // 2
-        remote(
-            plane_send.at[chip],
-            plane_recv.at[chip],
-            "context",
-            peer,
-            p_send.at[4, k],
-            p_recv.at[4, k],
-        ).wait_recv()
-        total = total + plane_recv[chip].astype(F32)
-    middle = model_width // 2
-    for i in range(spans):
-        v = total[i * rows_dev : (i + 1) * rows_dev]
-        last_send[i] = jnp.concatenate([v[:, :middle], v[:, middle:]], axis=0).astype(BF16)
-    z_scatter(last_send, last_recv, 4)
-    routed = z_scatter_sum(last_send, last_recv, 4)
-    routed = jnp.concatenate([routed[:rows_dev], routed[rows_dev:]], axis=1)
+    made_by = expert_up(bases[1])
+    for part in range(2):
+        expert_down(made_by, part, own_sum)
+        remote(*pair(part)).wait_recv()
+        for k in range(n - 2, 0, -2):
+            peer = xor(c, k)
+            chip = peer // 2
+            both = own_sum[part, chip].astype(F32) + pair_recv[part, chip].astype(F32)
+            plane_send[part, chip] = both.astype(BF16)
+            push(
+                plane_send.at[part, chip],
+                plane_recv.at[part, c // 2],
+                "context",
+                peer,
+                p_send.at[4 + part, k],
+                p_recv.at[4 + part, k],
+            )
+    quarter = middle // 2
+    for part in range(2):
+        total = own_sum[part, c // 2].astype(F32) + pair_recv[part, c // 2].astype(F32)
+        for k in range(2, n, 2):
+            peer = xor(c, k)
+            chip = peer // 2
+            remote(
+                plane_send.at[part, chip],
+                plane_recv.at[part, chip],
+                "context",
+                peer,
+                p_send.at[4 + part, k],
+                p_recv.at[4 + part, k],
+            ).wait_recv()
+            total = total + plane_recv[part, chip].astype(F32)
+        for i in range(spans):
+            v = total[i * rows_dev : (i + 1) * rows_dev]
+            last_send[part, i] = jnp.concatenate([v[:, :quarter], v[:, quarter:]], axis=0).astype(
+                BF16
+            )
+        z_scatter(last_send.at[part], last_recv.at[part], (4, 6)[part])
+    pieces = []
+    for part in range(2):
+        v = z_scatter_sum(last_send.at[part], last_recv.at[part], (4, 6)[part])
+        pieces += [v[:rows_dev], v[rows_dev:]]
+    routed = jnp.concatenate(pieces, axis=1)
     layer_out[...] = jnp.where(own_keep >= 0, resid + routed, 0.0).astype(BF16)
     for copy in pending:
         copy.wait_send()
@@ -516,30 +549,30 @@
             pltpu.VMEM((spans, keep_count, local_latent), F32),
             pltpu.VMEM((n, keep_count, key_width), BF16),
             pltpu.VMEM((n, keep_count, mixed_width), BF16),
-            pltpu.VMEM((spans, n * rows_dev, columns), BF16),
-            pltpu.VMEM((spans, n * rows_dev, columns), BF16),
+            pltpu.VMEM((2, spans, chips * rows_dev, columns), BF16),
+            pltpu.VMEM((2, spans, chips * rows_dev, columns), BF16),
             pltpu.VMEM((n, rows_dev, columns), F32),
             pltpu.VMEM((n, rows_dev, columns), F32),
             pltpu.VMEM((spans, 2 * rows_dev, half_width), BF16),
             pltpu.VMEM((n, keep_count, wide), BF16),
             pltpu.VMEM((many, hidden), F32),
             pltpu.VMEM((many, hidden), F32),
-            pltpu.VMEM((chips, keep_count, model_width), BF16),
-            pltpu.VMEM((chips, keep_count, model_width), BF16),
-            pltpu.VMEM((chips, keep_count, model_width), BF16),
-            pltpu.VMEM((chips, keep_count, model_width), BF16),
-            pltpu.VMEM((chips, keep_count, model_width), BF16),
-            pltpu.VMEM((spans, 2 * rows_dev, model_width // 2), BF16),
-            pltpu.VMEM((spans, 2 * rows_dev, model_width // 2), BF16),
+            pltpu.VMEM((2, chips, keep_count, model_width // 2), BF16),
+            pltpu.VMEM((2, chips, keep_count, model_width // 2), BF16),
+            pltpu.VMEM((2, chips, keep_count, model_width // 2), BF16),
+            pltpu.VMEM((2, chips, keep_count, model_width // 2), BF16),
+            pltpu.VMEM((2, chips, keep_count, model_width // 2), BF16),
+            pltpu.VMEM((2, spans, 2 * rows_dev, model_width // 4), BF16),
+            pltpu.VMEM((2, spans, 2 * rows_dev, model_width // 4), BF16),
             pltpu.SemaphoreType.DMA((5,)),
-            pltpu.SemaphoreType.DMA((5, spans)),
-            pltpu.SemaphoreType.DMA((5, spans)),
-            pltpu.SemaphoreType.DMA((5, n)),
-            pltpu.SemaphoreType.DMA((5, n)),
-            pltpu.SemaphoreType.DMA((2,)),
+            pltpu.SemaphoreType.DMA((7, spans)),
+            pltpu.SemaphoreType.DMA((7, spans)),
+            pltpu.SemaphoreType.DMA((6, n)),
+            pltpu.SemaphoreType.DMA((6, n)),
+            pltpu.SemaphoreType.DMA((2, 2)),
         ],
         compiler_params=pltpu.CompilerParams(
-            collective_id=0, has_side_effects=True, vmem_limit_bytes=53 * 1024 * 1024
+            collective_id=0, has_side_effects=True, vmem_limit_bytes=56 * 1024 * 1024
         ),
     )(
         raw_tokens,

time: 75.6 us -> 64.8 us (0.86)
  local copies, waits for them, and re-layouts: 8.61 us -> 2.77 us
  Pallas kernels: 65.9 us -> 60.6 us
    unnamed x22 -> x2, local copies, waits for them, and re-layouts: 8.61 us -> 2.77 us
    pallas_call x1, Pallas kernels: 65.9 us -> 60.6 us  [per_device(): pl.pallas_call(functools.partial(kernel, n, spans), out_shape=(jax.ShapeD...]
where the time goes in v3:
time: 64.8 us; the launch traced here: 64 us
  Pallas kernels  60.6 us (94%)
  local copies, waits for them, and re-layouts  2.77 us (4%)
    pallas_call x1, Pallas kernels, per_device(): pl.pallas_call(functools.partial(kernel, n, spans), out_shape=(jax.ShapeD...  60.6 us
    unnamed x2, local copies, waits for them, and re-layouts  2.77 us

profile of v3, /device:TPU:0, one launch (start us, length us, event | category | flops | bytes accessed | tf_op | source)
XLA Modules:
  0.0 64.0 jit_solution(6460165656961745668)
XLA Ops:
  0.6 60.6 %shard_map.149 = (bf16[8,2048]{1,0:T(8,128)(2,1)}, bf16[32,576]{1,0:T(8,128)(2,1)}) custom-call(bf16[192,512]{1,0:T(8,128)(2,1)} %raw.1, s32[1,32]{1,0:T(1,128)} %keep.1, f32[1,64]{1,0:T(1,128)} %constant.2.clone.freqs, f32[1,2048]{1,0:T(1,128)} %bitcast.8, f32[1,512]{1,0:T(1,128)} %bitcast.10, f32[1,2048]{1,0:T(1,128)} %bitcast.9, s32[8,6]{1,0:T(8,128)} %ids.1, ...), custom_call_target="tpu_custom_call" | custom-call | tf_op jit(solution)/shard_map/pallas_call | solution.py:532
  61.2 1.4 %copy.18 = bf16[8,2048]{1,0:T(8,128)(2,1)} copy(bf16[8,2048]{1,0:T(8,128)(2,1)} %get-tuple-element.4) | data formatting | bytes 65536
  62.6 1.4 %copy.19 = bf16[32,576]{1,0:T(8,128)(2,1)} copy(bf16[32,576]{1,0:T(8,128)(2,1)} %get-tuple-element.5) | data formatting | bytes 73728
